TPU v7x, 32 devices: a whole 2x2x4 slice. The times are simulated.
32 devices in a mesh: pipe: 2 (over x), tensor: 4 (over y, core), dp: 4 (over z).
Axes of the slice: x: 2, y: 2, z: 4, core: 2. Of those that a mesh axis runs over, the one named last changes fastest.
Arguments:
- fwd_qkv: bfloat16 [3, 8, 256, 8192], P(None, ('pipe', 'dp'), None, 'tensor'), may hold values from -8 to 8, as said below
- fwd_segments: int32 [8, 256], P(('pipe', 'dp')), may hold values from 0 to 15, as said below
- parked: bfloat16 [3, 8, 256, 8192], P(None, ('pipe', 'dp'), 'tensor'), may hold values from -8 to 8, as said below
- bwd_segments: int32 [8, 256], P(('pipe', 'dp')), may hold values from 0 to 15, as said below
- grad_out: bfloat16 [8, 256, 8192], P(('pipe', 'dp'), None, 'tensor'), may hold values from -6 to 6
- loss_tokens: int32 [8], P(('pipe', 'dp')), may hold values from 1 to 256
Outputs:
- received: bfloat16 [8, 256, 8192], P(('pipe', 'dp'), None, 'tensor')
- grads: bfloat16 [3, 8, 256, 8192], P(None, ('pipe', 'dp'), None, 'tensor')
Inputs may be any that keep to these rules, and one draw needn't show every extreme that they name: `fwd_qkv`: Real-valued. `parked`: Real-valued. `fwd_segments`: in each slot the numbers start at 0, never fall, and change only at positions that are multiples of 16. `bwd_segments`: in each slot the numbers start at 0, never fall, and change only at positions that are multiples of 16.
All inputs are finite; a program needn't handle non-finite values.
Results may differ from a plain program's by a relative error of at most 0.0051.
Values may be sent and summed in bfloat16 or wider, within the bound.
A program may use at most 128 MiB of HBM per device.

v0:
```python
import jax
import jax.numpy as jnp
from jax import lax
from jax.sharding import PartitionSpec as P

HEAD_DIM = 128
SEQ = 256


def shifted(array, axis, by):
    devices = lax.axis_size(axis)
    return lax.ppermute(array, axis, [(i, (i + by) % devices) for i in range(devices)])


def probabilities(query_heads, key_heads, segment):
    logits = jnp.einsum(
        "qhd,khd->hqk", query_heads, key_heads, preferred_element_type=jnp.float32
    ) * HEAD_DIM ** (-0.5)
    inside = segment[:, None] == segment[None, :]
    logits = jnp.where(inside[None], logits, jnp.float32(-1e30))
    highest = jnp.max(logits, axis=-1, keepdims=True)
    weights = jnp.exp(logits - highest)
    return weights / jnp.sum(weights, axis=-1, keepdims=True)


def split_rows(matrix):
    length = matrix.shape[0]
    return matrix.reshape(length, matrix.shape[1] // HEAD_DIM, HEAD_DIM)


def attend(queries, key_rows, value_rows, segment):
    probs_low = probabilities(split_rows(queries), split_rows(key_rows), segment).astype(
        jnp.bfloat16
    )
    mixed = jnp.einsum(
        "hqk,khd->qhd", probs_low, split_rows(value_rows), preferred_element_type=jnp.float32
    )
    return mixed.reshape(queries.shape).astype(jnp.bfloat16)


def attend_backward(queries, key_rows, value_rows, segment, upstream, factor):
    query_heads = split_rows(queries)
    key_heads = split_rows(key_rows)
    value_heads = split_rows(value_rows)
    upstream_heads = split_rows(upstream)
    stash_probs = probabilities(query_heads, key_heads, segment)
    stash_probs_low = stash_probs.astype(jnp.bfloat16)
    grad_value = jnp.einsum(
        "hqk,qhd->khd", stash_probs_low, upstream_heads, preferred_element_type=jnp.float32
    )
    grad_probs = jnp.einsum(
        "qhd,khd->hqk", upstream_heads, value_heads, preferred_element_type=jnp.float32
    )
    center = jnp.sum(stash_probs * grad_probs, axis=-1, keepdims=True)
    grad_logits = (stash_probs * (grad_probs - center) * HEAD_DIM ** (-0.5)).astype(jnp.bfloat16)
    grad_query = jnp.einsum(
        "hqk,khd->qhd", grad_logits, key_heads, preferred_element_type=jnp.float32
    )
    grad_key = jnp.einsum(
        "hqk,qhd->khd", grad_logits, query_heads, preferred_element_type=jnp.float32
    )
    stacked = jnp.stack([grad_query, grad_key, grad_value]) * factor
    return stacked.reshape(3, queries.shape[0], queries.shape[1]).astype(jnp.bfloat16)


def split_heads(parked_block):
    return lax.all_to_all(parked_block, "tensor", split_axis=3, concat_axis=2, tiled=True)


def fetch(parked_block):
    sections = lax.axis_size("pipe")
    leading = parked_block.shape[0]
    length = parked_block.shape[2]
    columns = parked_block.shape[3]
    pieces = parked_block.reshape(leading, sections, length // sections, columns)
    spread = lax.all_to_all(pieces, "pipe", split_axis=1, concat_axis=1, tiled=True)
    spread = jnp.flip(spread, axis=1)
    returned = lax.all_to_all(spread, "pipe", split_axis=1, concat_axis=1, tiled=True)
    return returned.reshape(leading, 1, length, columns)


def on_device(fwd_qkv, fwd_segments, parked, bwd_segments, grad_out, loss_tokens):
    forward_out = attend(fwd_qkv[0, 0], fwd_qkv[1, 0], fwd_qkv[2, 0], fwd_segments[0])
    received = shifted(forward_out[None], "pipe", 1)
    upstream = shifted(grad_out, "pipe", -1)
    token_total = lax.psum(jnp.sum(loss_tokens.astype(jnp.float32)), "dp")
    factor = jnp.float32(lax.axis_size("dp") * SEQ) / token_total
    stash = split_heads(fetch(parked))
    grads = attend_backward(
        stash[0, 0], stash[1, 0], stash[2, 0], bwd_segments[0], upstream[0], factor
    )
    return (received, grads[:, None])


def solution(mesh):
    placed = (
        P(None, ("pipe", "dp"), None, "tensor"),
        P(("pipe", "dp"), None),
        P(None, ("pipe", "dp"), "tensor", None),
        P(("pipe", "dp"), None),
        P(("pipe", "dp"), None, "tensor"),
        P(("pipe", "dp")),
    )
    return jax.shard_map(
        on_device,
        mesh=mesh,
        in_specs=placed,
        out_specs=(P(("pipe", "dp"), None, "tensor"), P(None, ("pipe", "dp"), None, "tensor")),
        check_vma=False,
    )
```

profile of v0, /device:TPU:0, one launch (start us, length us, event | category | flops | bytes accessed | tf_op | source)
XLA Modules:
  0.0 227.9 jit_solution(7652430891297713709)
XLA Ops:
  0.6 2.2 copy.94
  2.8 40.2 %all_to_all.25 = bf16[3,2,32,8192]{3,2,0,1:T(8,128)(2,1)S(1)} all-to-all(bf16[3,2,32,8192]{3,2,0,1:T(8,128)(2,1)S(1)} %copy.94), channel_id=1, replica_groups=mesh['pipe'=2,'tensor'=4,'dp'=4] {'pipe'}, dimensions={1} | all-to-all | bytes 6291456 | tf_op jit(solution)/shard_map/all_to_all | solution.py:76
  43.0 1.9 rev.4
  44.9 39.2 %all_to_all.26 = bf16[3,2,32,8192]{3,2,0,1:T(8,128)(2,1)S(1)} all-to-all(bf16[3,2,32,8192]{3,2,0,1:T(8,128)(2,1)} %rev.4), channel_id=1, replica_groups=mesh['pipe'=2,'tensor'=4,'dp'=4] {'pipe'}, dimensions={1} | all-to-all | bytes 6291456 | tf_op jit(solution)/shard_map/all_to_all | solution.py:78
  84.1 0.2 copy.95
  84.3 8.4 %copy.96 = bf16[3,1,64,8192]{2,0,1,3:T(4,128)(2,1)} copy(bf16[3,1,64,8192]{3,2,0,1:T(8,128)(2,1)S(1)} %bitcast.49) | data formatting | bytes 6291456 | tf_op jit(solution)/shard_map/reshape | solution.py:79
  92.7 8.6 %reshape.153 = bf16[4,2,196608]{2,1,0:T(2,128)(2,1)} reshape(bf16[8192,1,3,64]{3,2,1,0:T(4,128)(2,1)} %bitcast.46) | data formatting | bytes 6291456
  101.4 3.7 %all-to-all-start.2 = ((bf16[4,2,196608]{2,1,0:T(2,128)(2,1)}), bf16[4,2,196608]{2,1,0:T(2,128)(2,1)S(1)}, u32[]{:S(2)}, u32[]{:S(2)}) async-start(bf16[4,2,196608]{2,1,0:T(2,128)(2,1)} %reshape.153), calls=%async_computation.2 | async-start | bytes 6291456 | tf_op jit(solution)/shard_map/all_to_all | solution.py:67
  105.1 3.6 %fusion.42 = (bf16[1,1,256,2048]{3,2,1,0:T(8,128)(2,1)}, bf16[1,1,256,2048]{3,2,1,0:T(8,128)(2,1)}, bf16[1,1,256,2048]{3,2,1,0:T(8,128)(2,1)}) fusion(bf16[3,1,256,2048]{3,2,1,0:T(8,128)(2,1)} %param.6), kind=kLoop, calls=%fused_computation.45 | loop fusion | bytes 6291456 | tf_op jit(solution)/shard_map/slice | solution.py:83
  108.7 2.3 %copy.122 = bf16[1,1,256,2048]{2,3,1,0:T(8,128)(2,1)} copy(bf16[1,1,256,2048]{3,2,1,0:T(8,128)(2,1)} %get-tuple-element.6) | data formatting | bytes 2097152
  111.0 2.3 copy.123
  113.3 2.3 copy.91
  115.6 0.0 copy-done.2
  115.6 0.1 broadcast_compare_fusion.1
  115.7 5.0 %fusion.43 = (f32[16,256]{1,0:T(8,128)S(1)}, f32[16,256,256]{1,2,0:T(8,128)}) fusion(pred[256,256]{0,1:T(8,128)(4,1)S(1)} %broadcast_compare_fusion.1, bf16[256,16,128]{0,2,1:T(8,128)(2,1)} %bitcast.56, bf16[256,16,128]{0,2,1:T(8,128)(2,1)} %bitcast.58), kind=kOutput, calls=%fused_computation.46 | convolution fusion | flops 272630016 | bytes 6373376 | tf_op jit(solution)/shard_map/sub | solution.py:22
  120.7 4.0 %fusion.26 = bf16[16,256,128]{1,2,0:T(8,128)(2,1)} fusion(bf16[256,16,128]{0,2,1:T(8,128)(2,1)} %bitcast.57, f32[16,256,256]{1,2,0:T(8,128)} %get-tuple-element.9, f32[16,256]{1,0:T(8,128)S(1)} %get-tuple-element.8), kind=kOutput, calls=%fused_computation.29 | convolution fusion | flops 271056896 | bytes 6307840 | tf_op jit(solution)/shard_map/hqk,khd->qhd/dot_general | solution.py:35
  124.6 2.3 copy.93
  126.9 0.3 collective-permute-start
  127.2 2.3 %copy.102 = bf16[1,256,2048]{1,2,0:T(8,128)(2,1)} copy(bf16[1,256,2048]{2,1,0:T(8,128)(2,1)} %param.10) | data formatting | bytes 2097152 | tf_op args[4]
  129.5 1.7 collective-permute-start.1
  131.9 13.8 %psum.7 = f32[]{:T(128)} all-reduce(f32[]{:T(128)} %bitcast.18), channel_id=1, replica_groups=mesh['pipe'=2,'tensor'=4,'dp'=4] {'dp'}, use_global_device_ids=true, to_apply=%region_5.6 | all-reduce | flops 1 | bytes 8 | tf_op jit(solution)/shard_map/psum | solution.py:86
  146.5 0.0 copy-done.3
  146.5 0.1 broadcast_compare_fusion
  146.6 6.6 %collective-permute-done = bf16[1,256,2048]{2,1,0:T(8,128)(2,1)} collective-permute-done((bf16[1,256,2048]{2,1,0:T(8,128)(2,1)}, bf16[1,256,2048]{2,1,0:T(8,128)(2,1)}, u32[]{:S(2)}, u32[]{:S(2)}) %collective-permute-start) | collective-permute-done | bytes 1048608 | tf_op jit(solution)/shard_map/ppermute | solution.py:12
  153.2 0.0 all-to-all-done.2
  153.2 6.4 %reshape.154 = bf16[8192,1,3,64]{3,2,1,0:T(4,128)(2,1)} reshape(bf16[4,2,196608]{2,1,0:T(2,128)(2,1)S(1)} %all-to-all-done.2) | data formatting | bytes 6291456
  159.5 12.0 %copy.121 = bf16[3,1,64,4,2048]{4,3,2,0,1:T(4,128)(2,1)S(1)} copy(bf16[3,1,64,4,2048]{2,0,4,3,1:T(4,128)(2,1)} %bitcast.47) | data formatting | bytes 6291456 | tf_op jit(solution)/shard_map/all_to_all | solution.py:67
  171.6 2.8 %fusion.41 = (bf16[1,1,4,64,2048]{4,2,3,0,1:T(4,128)(2,1)}, bf16[1,1,4,64,2048]{4,2,3,0,1:T(4,128)(2,1)}, bf16[1,1,4,64,2048]{4,2,3,0,1:T(4,128)(2,1)}) fusion(bf16[3,1,4,64,2048]{4,2,3,0,1:T(4,128)(2,1)S(1)} %bitcast.48), kind=kLoop, calls=%fused_computation.44 | loop fusion | bytes 6291456 | tf_op jit(solution)/shard_map/slice | solution.py:90
  174.4 3.4 %copy.124 = bf16[1,1,4,64,2048]{3,2,4,1,0:T(4,128)(2,1)S(1)} copy(bf16[1,1,4,64,2048]{4,2,3,0,1:T(4,128)(2,1)} %get-tuple-element.3) | data formatting | bytes 2097152 | tf_op jit(solution)/shard_map/reshape;squeeze | solution.py:28
  177.8 2.2 reshape.151
  179.9 0.0 copy-done
  179.9 1.7 copy.125
  181.6 1.4 reshape.152
  183.0 1.8 copy.103
  184.8 0.0 copy-start.1
  184.8 0.2 copy.128
  185.0 0.0 collective-permute-done.1
  185.0 3.9 %fusion.27 = f32[16,256,256]{1,2,0:T(8,128)} fusion(bf16[256,16,128]{0,2,1:T(8,128)(2,1)} %bitcast.11, bf16[256,16,128]{2,1,0:T(8,128)(2,1)S(1)} %bitcast.51), kind=kOutput, calls=%fused_computation.30 | convolution fusion | flops 268435456 | bytes 6291456 | tf_op jit(solution)/shard_map/qhd,khd->hqk/dot_general | solution.py:51
  189.0 0.0 copy-done.1
  189.0 3.4 %fusion.44 = (f32[16,256]{1,0:T(8,128)S(1)}, f32[16,256,256]{1,2,0:T(8,128)}) fusion(pred[256,256]{0,1:T(8,128)(4,1)S(1)} %broadcast_compare_fusion, bf16[256,16,128]{0,2,1:T(8,128)(2,1)S(1)} %reshape.152, bf16[256,16,128]{0,2,1:T(8,128)(2,1)S(1)} %copy-done.1), kind=kOutput, calls=%fused_computation.47 | convolution fusion | flops 272630016 | bytes 6373376 | tf_op jit(solution)/shard_map/sub | solution.py:22
  192.4 8.5 %fusion.13 = f32[16,256,128]{1,2,0:T(8,128)} fusion(bf16[256,16,128]{0,2,1:T(8,128)(2,1)S(1)} %copy-done.1, f32[16,256,256]{1,2,0:T(8,128)} %fusion.27, f32[16,256,256]{1,2,0:T(8,128)} %get-tuple-element.11, f32[16,256]{1,0:T(8,128)S(1)} %get-tuple-element.10), kind=kOutput, calls=%fused_computation.16 | convolution fusion | flops 275779840 | bytes 11550720 | tf_op jit(solution)/shard_map/hqk,khd->qhd/dot_general | solution.py:56
  200.9 8.6 %fusion.10 = f32[16,256,128]{1,2,0:T(8,128)} fusion(bf16[256,16,128]{0,2,1:T(8,128)(2,1)S(1)} %reshape.152, f32[16,256,256]{1,2,0:T(8,128)} %fusion.27, f32[16,256,256]{1,2,0:T(8,128)} %get-tuple-element.11, f32[16,256]{1,0:T(8,128)S(1)} %get-tuple-element.10), kind=kOutput, calls=%fused_computation.15 | convolution fusion | flops 275779840 | bytes 11550720 | tf_op jit(solution)/shard_map/hqk,qhd->khd/dot_general | solution.py:59
  209.6 4.6 %fusion.15 = f32[16,256,128]{1,2,0:T(8,128)} fusion(bf16[256,16,128]{0,2,1:T(8,128)(2,1)} %bitcast.11, f32[16,256,256]{1,2,0:T(8,128)} %get-tuple-element.11, f32[16,256]{1,0:T(8,128)S(1)} %get-tuple-element.10), kind=kOutput, calls=%fused_computation.17 | convolution fusion | flops 270532608 | bytes 7356416 | tf_op jit(solution)/shard_map/hqk,qhd->khd/dot_general | solution.py:48
  214.2 1.9 copy.111
  216.1 3.0 %copy.112 = f32[1,1,256,2048]{3,2,1,0:T(8,128)} copy(f32[1,1,256,2048]{2,3,1,0:T(8,128)} %bitcast.54) | data formatting | bytes 4194304 | tf_op jit(solution)/shard_map/stack | solution.py:62
  219.1 2.9 %copy.113 = f32[1,1,256,2048]{3,2,1,0:T(8,128)} copy(f32[1,1,256,2048]{2,3,1,0:T(8,128)} %bitcast.55) | data formatting | bytes 4194304 | tf_op jit(solution)/shard_map/stack | solution.py:62
  222.0 3.6 %fusion.3 = bf16[3,1,256,2048]{3,2,1,0:T(8,128)(2,1)} fusion(f32[1,1,256,2048]{3,2,1,0:T(8,128)} %copy.113, f32[1,1,256,2048]{3,2,1,0:T(8,128)} %copy.112, f32[1,1,256,2048]{3,2,1,0:T(8,128)S(1)} %copy.111, f32[]{:T(128)S(6)} %div.23), kind=kLoop, calls=%fused_computation.4 | loop fusion | flops 6291456 | bytes 9437188 | tf_op jit(solution)/shard_map/convert_element_type | solution.py:63
  225.6 2.3 %copy.133 = bf16[1,256,2048]{2,1,0:T(8,128)(2,1)} copy(bf16[1,256,2048]{2,1,0:T(8,128)(2,1)} %collective-permute-done) | data formatting | bytes 2097152
  (3 shorter events, 0.0 us)
Async XLA Ops:
  101.4 51.8 %all-to-all-start.2 = ((bf16[4,2,196608]{2,1,0:T(2,128)(2,1)}), bf16[4,2,196608]{2,1,0:T(2,128)(2,1)S(1)}, u32[]{:S(2)}, u32[]{:S(2)}) async-start(bf16[4,2,196608]{2,1,0:T(2,128)(2,1)} %reshape.153), calls=%async_computation.2 | async-start | bytes 6291456 | tf_op jit(solution)/shard_map/all_to_all | solution.py:67
  108.7 6.8 %copy-start.2 = (s32[1,256]{1,0:T(1,128)S(1)}, s32[1,256]{1,0:T(1,128)}, u32[]{:S(2)}) copy-start(s32[1,256]{1,0:T(1,128)} %param.7) | copy-start | bytes 3076
  124.6 21.8 %copy-start.3 = (s32[1,256]{1,0:T(1,128)S(1)}, s32[1,256]{1,0:T(1,128)}, u32[]{:S(2)}) copy-start(s32[1,256]{1,0:T(1,128)} %param.9) | copy-start | bytes 3076
  126.9 26.3 %collective-permute-start = (bf16[1,256,2048]{2,1,0:T(8,128)(2,1)}, bf16[1,256,2048]{2,1,0:T(8,128)(2,1)}, u32[]{:S(2)}, u32[]{:S(2)}) collective-permute-start(bf16[1,256,2048]{2,1,0:T(8,128)(2,1)} %copy.93), channel_id=1, source_target_pairs={{0,16},{16,0},{1,17},{17,1},{2,18},{18,2},{3,19},{19,3},{4,20},{20... | collective-permute-start | bytes 3145736 | tf_op jit(solution)/shard_map/ppermute | solution.py:12
  129.5 55.5 %collective-permute-start.1 = (bf16[1,256,2048]{1,2,0:T(8,128)(2,1)}, bf16[1,256,2048]{1,2,0:T(8,128)(2,1)}, u32[]{:S(2)}, u32[]{:S(2)}) collective-permute-start(bf16[1,256,2048]{1,2,0:T(8,128)(2,1)} %copy.102), channel_id=1, source_target_pairs={{0,16},{16,0},{1,17},{17,1},{2,18},{18,2},{3,19},{19,3},{4,20},{20... | collective-permute-start | bytes 3145736 | tf_op jit(solution)/shard_map/ppermute | solution.py:12
  174.4 5.5 %copy-start = (bf16[1,1,4,64,2048]{4,2,3,0,1:T(4,128)(2,1)S(1)}, bf16[1,1,4,64,2048]{4,2,3,0,1:T(4,128)(2,1)}, u32[]{:S(2)}) copy-start(bf16[1,1,4,64,2048]{4,2,3,0,1:T(4,128)(2,1)} %get-tuple-element.4) | copy-start | bytes 3145732
  184.8 4.2 %copy-start.1 = (bf16[256,16,128]{0,2,1:T(8,128)(2,1)S(1)}, bf16[256,16,128]{0,2,1:T(8,128)(2,1)}, u32[]{:S(2)}) copy-start(bf16[256,16,128]{0,2,1:T(8,128)(2,1)} %reshape.151) | copy-start | bytes 3145732
where the time goes:
time: 229 us; the launch traced here: 228 us
  blocking collectives  93.2 us (41%)
  local copies, waits for them, and re-layouts  78.3 us (34%)
  matrix products  38.1 us (17%)
  waiting for transfers between devices  6.6 us (3%)
  starting transfers between devices  5.73 us (3%)
  other arithmetic  3.84 us (2%)
    all_to_all x1, blocking collectives, fetch(): lax.all_to_all(pieces, 'pipe', split_axis=1, concat_axis=1, tiled=True)  40.2 us
    all_to_all x1, blocking collectives, fetch(): lax.all_to_all(spread, 'pipe', split_axis=1, concat_axis=1, tiled=True)  39.2 us
    unnamed x15, local copies, waits for them, and re-layouts  24.4 us
    psum x1, blocking collectives, on_device(): token_total = lax.psum(jnp.sum(loss_tokens.astype(jnp.float32)), 'dp')  13.8 us
    all_to_all x1, local copies, waits for them, and re-layouts, split_heads(): lax.all_to_all(parked_block, 'tensor', split_axis=3, concat_axis=2, tiled...  12 us
    dot_general x1, matrix products, attend_backward(): jnp.einsum('hqk,qhd->khd', grad_logits, query_heads, preferred_element_ty...  8.63 us
    another operation x4, local copies, waits for them, and re-layouts, split_rows(): return matrix.reshape(length, matrix.shape[1] // HEAD_DIM, HEAD_DIM)  8.55 us
    dot_general x1, matrix products, attend_backward(): jnp.einsum('hqk,khd->qhd', grad_logits, key_heads, preferred_element_type...  8.5 us
  transfers between devices with their start and end apart: 3, of which 1 were waited for; matrix products, arithmetic and copies ran while one was open for 25% of the time, Pallas kernels for 0%

commit v1 on v0

v1 whole, which is shorter than its diff:
```python
import functools

import jax
import jax.numpy as jnp
from jax import lax
from jax.experimental import pallas as pl
from jax.experimental.pallas import tpu as pltpu
from jax.sharding import PartitionSpec as P

HEAD_DIM = 128
SCALE = HEAD_DIM ** (-0.5)
GROUP = 2
MESH = pl.DeviceIdType.MESH


def dot(a, b, contract):
    return lax.dot_general(a, b, (contract, ((), ())), preferred_element_type=jnp.float32)


def softmax(query, key, bias):
    logits = dot(query, key, ((1,), (1,))) * SCALE + bias
    weights = jnp.exp(logits - jnp.max(logits, axis=-1, keepdims=True))
    return weights / jnp.sum(weights, axis=-1, keepdims=True)


def mask_bias(segment):
    length = segment.shape[1]
    along = jnp.broadcast_to(segment.astype(jnp.float32), (length, length))
    return jnp.where(along == along.T, jnp.float32(0), jnp.float32(-1e30))


def kernel(
    sections, tensors, replicas,
    fwd_hbm, fwd_seg_hbm, parked_hbm, bwd_seg_hbm, up_hbm, tokens_hbm,
    received_hbm, grads_hbm,
    fwd, out, stash, up, grads, fwd_bias, bwd_bias, fwd_seg, bwd_seg, tokens, token_tile, token_all,
    fwd_sem, up_sem, own_sem, small_sem,
    part_send, part_recv, out_send, out_recv, grad_send, grad_recv,
    seg_send, seg_recv, tok_send, tok_recv,
):
    section = lax.axis_index("pipe")
    lane = lax.axis_index("tensor")
    replica = lax.axis_index("dp")
    after = lax.rem(section + 1, sections)
    before = lax.rem(section + sections - 1, sections)
    mirror = sections - 1 - section
    length = fwd.shape[1]
    width = GROUP * HEAD_DIM
    columns = fwd.shape[2]
    groups = columns // width
    rows = parked_hbm.shape[2]

    barrier = pltpu.get_barrier_semaphore()
    greeted = 0
    for step in range(1, tensors):
        pl.semaphore_signal(barrier, inc=1, device_id={"tensor": lax.rem(lane + step, tensors)}, device_id_type=MESH)
        greeted += 1
    for other in range(replicas):
        pl.semaphore_signal(barrier, inc=1, device_id={"pipe": mirror, "dp": other}, device_id_type=MESH)
        greeted += 1
    if sections > 2:
        for other in (after, before):
            pl.semaphore_signal(barrier, inc=1, device_id={"pipe": other}, device_id_type=MESH)
            greeted += 1

    def span(g):
        return pl.ds(pl.multiple_of(g * width, width), width)

    def load_fwd(g):
        return pltpu.make_async_copy(fwd_hbm.at[:, 0, :, span(g)], fwd.at[:, :, span(g)], fwd_sem.at[g])

    def load_up(g):
        return pltpu.make_async_copy(up_hbm.at[0, :, span(g)], up.at[:, span(g)], up_sem.at[g])

    def my_rows(who):
        return pl.ds(pl.multiple_of(who * rows, rows), rows)

    def parked_span(who, g):
        return pl.ds(pl.multiple_of(who * columns + g * width, width), width)

    def load_own(g):
        return pltpu.make_async_copy(
            parked_hbm.at[:, 0, :, parked_span(lane, g)], stash.at[:, my_rows(lane), span(g)], own_sem.at[g]
        )

    def send_part(step, g):
        other = lax.rem(lane + step, tensors)
        return pltpu.make_async_remote_copy(
            src_ref=parked_hbm.at[:, 0, :, parked_span(other, g)],
            dst_ref=stash.at[:, my_rows(lane), span(g)],
            send_sem=part_send.at[step - 1, g],
            recv_sem=part_recv.at[step - 1, g],
            device_id={"tensor": other},
            device_id_type=MESH,
        )

    def recv_part(step, g):
        other = lax.rem(lane + tensors - step, tensors)
        return pltpu.make_async_remote_copy(
            src_ref=parked_hbm.at[:, 0, :, parked_span(lane, g)],
            dst_ref=stash.at[:, my_rows(other), span(g)],
            send_sem=part_send.at[step - 1, g],
            recv_sem=part_recv.at[step - 1, g],
            device_id={"tensor": other},
            device_id_type=MESH,
        )

    def send_out(g):
        return pltpu.make_async_remote_copy(
            src_ref=out.at[:, span(g)],
            dst_ref=received_hbm.at[0, :, span(g)],
            send_sem=out_send.at[g],
            recv_sem=out_recv.at[g],
            device_id={"pipe": after},
            device_id_type=MESH,
        )

    def send_grads(g):
        return pltpu.make_async_remote_copy(
            src_ref=grads.at[:, :, span(g)],
            dst_ref=grads_hbm.at[:, 0, :, span(g)],
            send_sem=grad_send.at[g],
            recv_sem=grad_recv.at[g],
            device_id={"pipe": mirror},
            device_id_type=MESH,
        )

    def send_tokens(other, mine):
        return pltpu.make_async_remote_copy(
            src_ref=token_tile,
            dst_ref=token_all.at[mine],
            send_sem=tok_send.at[other],
            recv_sem=tok_recv.at[mine],
            device_id={"pipe": mirror, "dp": other},
            device_id_type=MESH,
        )

    send_segment = pltpu.make_async_remote_copy(
        src_ref=bwd_seg_hbm,
        dst_ref=bwd_seg,
        send_sem=seg_send,
        recv_sem=seg_recv,
        device_id={"pipe": mirror},
        device_id_type=MESH,
    )

    seg_copy = pltpu.make_async_copy(fwd_seg_hbm, fwd_seg, small_sem.at[0])
    tok_copy = pltpu.make_async_copy(tokens_hbm, tokens, small_sem.at[1])
    seg_copy.start()
    tok_copy.start()
    pl.loop(0, groups)(lambda g: load_fwd(g).start())
    pl.loop(0, groups)(lambda g: load_own(g).start())
    pl.loop(0, groups)(lambda g: load_up(g).start())

    def forward(g):
        load_fwd(g).wait()
        for h in range(GROUP):
            cols = pl.ds(pl.multiple_of(g * width + h * HEAD_DIM, HEAD_DIM), HEAD_DIM)
            probs = softmax(fwd[0, :, cols], fwd[1, :, cols], fwd_bias[...])
            mixed = dot(probs.astype(jnp.bfloat16), fwd[2, :, cols], ((1,), (0,)))
            out[:, cols] = mixed.astype(jnp.bfloat16)

    tok_copy.wait()
    token_tile[...] = jnp.full(token_tile.shape, tokens[0], jnp.int32)

    pl.semaphore_wait(barrier, greeted)
    send_segment.start()
    for other in range(replicas):
        send_tokens(other, replica).start()

    @pl.loop(0, groups)
    def _(g):
        for step in range(1, tensors):
            send_part(step, g).start()

    seg_copy.wait()
    fwd_bias[...] = mask_bias(fwd_seg[...])

    @pl.loop(0, groups)
    def _(g):
        forward(g)
        send_out(g).start()

    send_segment.wait()
    bwd_bias[...] = mask_bias(bwd_seg[...])
    total = jnp.zeros((1, HEAD_DIM), jnp.float32)
    for other in range(replicas):
        send_tokens(other, other).wait_recv()
        total += token_all[other, 0:1, :].astype(jnp.float32)
    factor = jnp.float32(replicas * length) / total

    @pl.loop(0, groups)
    def _(g):
        load_own(g).wait()
        load_up(g).wait()
        for step in range(1, tensors):
            recv_part(step, g).wait_recv()
        for h in range(GROUP):
            cols = pl.ds(pl.multiple_of(g * width + h * HEAD_DIM, HEAD_DIM), HEAD_DIM)
            query, key, value, upstream = stash[0, :, cols], stash[1, :, cols], stash[2, :, cols], up[:, cols]
            probs = softmax(query, key, bwd_bias[...])
            grad_value = dot(probs.astype(jnp.bfloat16), upstream, ((0,), (0,)))
            grad_probs = dot(upstream, value, ((1,), (1,)))
            center = jnp.sum(probs * grad_probs, axis=-1, keepdims=True)
            grad_logits = (probs * (grad_probs - center) * SCALE).astype(jnp.bfloat16)
            grad_query = dot(grad_logits, key, ((1,), (0,)))
            grad_key = dot(grad_logits, query, ((0,), (0,)))
            grads[0, :, cols] = (grad_query * factor).astype(jnp.bfloat16)
            grads[1, :, cols] = (grad_key * factor).astype(jnp.bfloat16)
            grads[2, :, cols] = (grad_value * factor).astype(jnp.bfloat16)
        send_grads(g).start()

    for other in range(replicas):
        send_tokens(other, replica).wait_send()

    @pl.loop(0, groups)
    def _(g):
        for step in range(1, tensors):
            send_part(step, g).wait_send()
        send_out(g).wait()

    @pl.loop(0, groups)
    def _(g):
        send_grads(g).wait()


def on_device(fwd_qkv, fwd_segments, parked, bwd_segments, grad_out, loss_tokens):
    sections = lax.axis_size("pipe")
    tensors = lax.axis_size("tensor")
    replicas = lax.axis_size("dp")
    length, columns = fwd_qkv.shape[2], fwd_qkv.shape[3]
    groups = columns // (GROUP * HEAD_DIM)
    if sections > 2:
        grad_out = lax.ppermute(grad_out, "pipe", [(i, (-i) % sections) for i in range(sections)])
    dma = pltpu.SemaphoreType.DMA
    received, grads = pl.pallas_call(
        functools.partial(kernel, sections, tensors, replicas),
        out_shape=(
            jax.ShapeDtypeStruct((1, length, columns), jnp.bfloat16),
            jax.ShapeDtypeStruct((3, 1, length, columns), jnp.bfloat16),
        ),
        in_specs=[pl.BlockSpec(memory_space=pl.ANY)] * 6,
        out_specs=(pl.BlockSpec(memory_space=pl.ANY), pl.BlockSpec(memory_space=pl.ANY)),
        scratch_shapes=[
            pltpu.VMEM((3, length, columns), jnp.bfloat16),
            pltpu.VMEM((length, columns), jnp.bfloat16),
            pltpu.VMEM((3, length, columns), jnp.bfloat16),
            pltpu.VMEM((length, columns), jnp.bfloat16),
            pltpu.VMEM((3, length, columns), jnp.bfloat16),
            pltpu.VMEM((length, length), jnp.float32),
            pltpu.VMEM((length, length), jnp.float32),
            pltpu.VMEM((1, length), jnp.int32),
            pltpu.VMEM((1, length), jnp.int32),
            pltpu.SMEM((1,), jnp.int32),
            pltpu.VMEM((8, HEAD_DIM), jnp.int32),
            pltpu.VMEM((replicas, 8, HEAD_DIM), jnp.int32),
            dma((groups,)), dma((groups,)), dma((groups,)), dma((2,)),
            dma((tensors - 1, groups)), dma((tensors - 1, groups)),
            dma((groups,)), dma((groups,)), dma((groups,)), dma((groups,)),
            dma, dma, dma((replicas,)), dma((replicas,)),
        ],
        compiler_params=pltpu.CompilerParams(
            collective_id=0, has_side_effects=True, vmem_limit_bytes=48 * 1024 * 1024
        ),
        cost_estimate=pl.CostEstimate(
            flops=14 * length * length * columns, bytes_accessed=22 * length * columns, transcendentals=0
        ),
    )(fwd_qkv, fwd_segments, parked, bwd_segments, grad_out, loss_tokens)
    return received, grads


def solution(mesh):
    placed = (
        P(None, ("pipe", "dp"), None, "tensor"),
        P(("pipe", "dp"), None),
        P(None, ("pipe", "dp"), "tensor", None),
        P(("pipe", "dp"), None),
        P(("pipe", "dp"), None, "tensor"),
        P(("pipe", "dp")),
    )
    return jax.shard_map(
        on_device,
        mesh=mesh,
        in_specs=placed,
        out_specs=(P(("pipe", "dp"), None, "tensor"), P(None, ("pipe", "dp"), None, "tensor")),
        check_vma=False,
    )
```

time: 229 us -> 106 us (0.46)
  Pallas kernels: 0 us -> 99.2 us
  blocking collectives: 93.2 us -> 0 us
  local copies, waits for them, and re-layouts: 78.3 us -> 5.21 us
  matrix products: 38.1 us -> 0 us
  waiting for transfers between devices: 6.6 us -> 0 us
  starting transfers between devices: 5.73 us -> 0 us
  other arithmetic: 3.84 us -> 0 us
    pallas_call x0 -> x1, Pallas kernels: none -> 99.2 us  [on_device(): pl.pallas_call(functools.partial(kernel, sections, tensors, replicas), ou...]
    all_to_all x2 -> x0, blocking collectives: 79.4 us -> none  [the longest x1 40.2 us: fetch(): lax.all_to_all(pieces, 'pipe', split_axis=1, concat_axis=1, tiled=True)]
    dot_general x5 -> x0, matrix products: 29.7 us -> none  [the longest x1 8.63 us: attend_backward(): jnp.einsum('hqk,qhd->khd', grad_logits, query_heads, preferred_element_ty...]
    unnamed x15 -> x8, local copies, waits for them, and re-layouts: 24.4 us -> 5.21 us
    another operation x7 -> x0, local copies, waits for them, and re-layouts: 16.3 us -> none  [the longest x4 8.55 us: split_rows(): return matrix.reshape(length, matrix.shape[1] // HEAD_DIM, HEAD_DIM)]
    psum x1 -> x0, blocking collectives: 13.8 us -> none  [on_device(): token_total = lax.psum(jnp.sum(loss_tokens.astype(jnp.float32)), 'dp')]
    all_to_all x2 -> x0, local copies, waits for them, and re-layouts: 12.2 us -> none  [the longest x1 12 us: split_heads(): lax.all_to_all(parked_block, 'tensor', split_axis=3, concat_axis=2, tiled...]
    reshape x2 -> x0, local copies, waits for them, and re-layouts: 10.6 us -> none  [the longest x1 8.43 us: fetch(): return returned.reshape(leading, 1, length, columns)]
  transfers between devices with their start and end apart: 3 -> 0, of which waited for: 1 -> 0; matrix products, arithmetic and copies ran while one was open for 25% -> 0% of each run, Pallas kernels for 0% -> 0%
where the time goes in v1:
time: 106 us
  Pallas kernels  99.2 us (94%)
  local copies, waits for them, and re-layouts  5.21 us (5%)
  between operations  1.3 us (1%)
    pallas_call x1, Pallas kernels, on_device(): pl.pallas_call(functools.partial(kernel, sections, tensors, replicas), ou...  99.2 us
    unnamed x8, local copies, waits for them, and re-layouts  5.21 us

profile of v1, /device:TPU:0, one launch (start us, length us, event | category | flops | bytes accessed | tf_op | source)
XLA Modules:
  0.0 105.7 jit_solution(730744031368047332)
XLA Ops:
  1.3 0.0 copy-start
  1.3 1.2 %copy-done = bf16[1,256,2048]{2,1,0:T(8,128)(2,1)S(1)} copy-done((bf16[1,256,2048]{2,1,0:T(8,128)(2,1)S(1)}, bf16[1,256,2048]{2,1,0:T(8,128)(2,1)}, u32[]{:S(2)}) %copy-start) | copy-done | bytes 1048600
  2.5 0.0 copy-start.1
  2.5 0.7 copy-done.1
  3.2 0.0 copy-start.2
  3.2 0.7 copy-done.2
  3.9 99.2 %shard_map.77 = (bf16[1,256,2048]{2,1,0:T(8,128)(2,1)S(1)}, bf16[3,1,256,2048]{3,2,1,0:T(8,128)(2,1)S(1)}) custom-call(bf16[3,1,256,2048]{3,2,1,0:T(8,128)(2,1)} %fwd_hbm.1, s32[1,256]{1,0:T(1,128)S(1)} %copy-done.1, bf16[3,1,64,8192]{3,2,1,0:T(8,128)(2,1)} %parked_hbm.1, s32[1,256]{1,0:T(1,128)S(1)} %copy-done.2, bf16[1,256,2048]{2,1,0:T(8,128)(2,1)S(1)} %copy-done, ...), custom_call_target="tpu_custom_call" | custom-call | flops 1879048192 | bytes 11534336 | tf_op jit(solution)/shard_map/pallas_call | solution.py:236
  103.1 1.0 copy.11
  104.0 1.7 %copy.12 = bf16[3,1,256,2048]{3,2,1,0:T(8,128)(2,1)} copy(bf16[3,1,256,2048]{3,2,1,0:T(8,128)(2,1)S(1)} %get-tuple-element.5) | data formatting | bytes 6291456
Async XLA Ops:
  1.3 1.2 %copy-start = (bf16[1,256,2048]{2,1,0:T(8,128)(2,1)S(1)}, bf16[1,256,2048]{2,1,0:T(8,128)(2,1)}, u32[]{:S(2)}) copy-start(bf16[1,256,2048]{2,1,0:T(8,128)(2,1)} %up_hbm.1) | copy-start | bytes 3145732
  2.5 0.7 copy-start.1
  3.2 0.7 copy-start.2

commit v2 on v1

--- a/solution.py
+++ b/solution.py
@@ -10,6 +10,7 @@
 HEAD_DIM = 128
 SCALE = HEAD_DIM ** (-0.5)
 GROUP = 2
+AHEAD = 2
 MESH = pl.DeviceIdType.MESH
 
 
@@ -163,20 +164,24 @@
     tok_copy.wait()
     token_tile[...] = jnp.full(token_tile.shape, tokens[0], jnp.int32)
 
+    seg_copy.wait()
+    fwd_bias[...] = mask_bias(fwd_seg[...])
+    forward(0)
+
     pl.semaphore_wait(barrier, greeted)
+    send_out(0).start()
     send_segment.start()
     for other in range(replicas):
         send_tokens(other, replica).start()
 
-    @pl.loop(0, groups)
-    def _(g):
+    def exchange(g):
         for step in range(1, tensors):
             send_part(step, g).start()
 
-    seg_copy.wait()
-    fwd_bias[...] = mask_bias(fwd_seg[...])
-
-    @pl.loop(0, groups)
+    for g in range(AHEAD):
+        exchange(g)
+
+    @pl.loop(1, groups)
     def _(g):
         forward(g)
         send_out(g).start()
@@ -195,6 +200,11 @@
         load_up(g).wait()
         for step in range(1, tensors):
             recv_part(step, g).wait_recv()
+
+        @pl.when(g < groups - AHEAD)
+        def _():
+            exchange(g + AHEAD)
+
         for h in range(GROUP):
             cols = pl.ds(pl.multiple_of(g * width + h * HEAD_DIM, HEAD_DIM), HEAD_DIM)
             query, key, value, upstream = stash[0, :, cols], stash[1, :, cols], stash[2, :, cols], up[:, cols]
@@ -239,7 +249,7 @@
             jax.ShapeDtypeStruct((1, length, columns), jnp.bfloat16),
             jax.ShapeDtypeStruct((3, 1, length, columns), jnp.bfloat16),
         ),
-        in_specs=[pl.BlockSpec(memory_space=pl.ANY)] * 6,
+        in_specs=[pl.BlockSpec(memory_space=pltpu.HBM)] * 6,
         out_specs=(pl.BlockSpec(memory_space=pl.ANY), pl.BlockSpec(memory_space=pl.ANY)),
         scratch_shapes=[
             pltpu.VMEM((3, length, columns), jnp.bfloat16),

time: 106 us -> 105 us (level)
  no operation moved by 1% of the time
where the time goes in v2:
time: 105 us
  Pallas kernels  98.2 us (94%)
  local copies, waits for them, and re-layouts  5.21 us (5%)
  between operations  1.3 us (1%)
    pallas_call x1, Pallas kernels, on_device(): pl.pallas_call(functools.partial(kernel, sections, tensors, replicas), ou...  98.2 us
    unnamed x8, local copies, waits for them, and re-layouts  5.21 us

profile of v2, /device:TPU:0, one launch (start us, length us, event | category | flops | bytes accessed | tf_op | source)
XLA Modules:
  0.0 104.7 jit_solution(6487269631991132818)
XLA Ops:
  1.3 0.0 copy-start
  1.3 1.2 %copy-done = bf16[1,256,2048]{2,1,0:T(8,128)(2,1)S(1)} copy-done((bf16[1,256,2048]{2,1,0:T(8,128)(2,1)S(1)}, bf16[1,256,2048]{2,1,0:T(8,128)(2,1)}, u32[]{:S(2)}) %copy-start) | copy-done | bytes 1048600
  2.5 0.0 copy-start.1
  2.5 0.7 copy-done.1
  3.2 0.0 copy-start.2
  3.2 0.7 copy-done.2
  3.9 98.2 %shard_map.77 = (bf16[1,256,2048]{2,1,0:T(8,128)(2,1)S(1)}, bf16[3,1,256,2048]{3,2,1,0:T(8,128)(2,1)S(1)}) custom-call(bf16[3,1,256,2048]{3,2,1,0:T(8,128)(2,1)} %fwd_hbm.1, s32[1,256]{1,0:T(1,128)S(1)} %copy-done.1, bf16[3,1,64,8192]{3,2,1,0:T(8,128)(2,1)} %parked_hbm.1, s32[1,256]{1,0:T(1,128)S(1)} %copy-done.2, bf16[1,256,2048]{2,1,0:T(8,128)(2,1)S(1)} %copy-done, ...), custom_call_target="tpu_custom_call" | custom-call | flops 1879048192 | bytes 11534336 | tf_op jit(solution)/shard_map/pallas_call | solution.py:246
  102.1 1.0 copy.11
  103.1 1.7 %copy.12 = bf16[3,1,256,2048]{3,2,1,0:T(8,128)(2,1)} copy(bf16[3,1,256,2048]{3,2,1,0:T(8,128)(2,1)S(1)} %get-tuple-element.5) | data formatting | bytes 6291456
Async XLA Ops:
  1.3 1.2 %copy-start = (bf16[1,256,2048]{2,1,0:T(8,128)(2,1)S(1)}, bf16[1,256,2048]{2,1,0:T(8,128)(2,1)}, u32[]{:S(2)}) copy-start(bf16[1,256,2048]{2,1,0:T(8,128)(2,1)} %up_hbm.1) | copy-start | bytes 3145732
  2.5 0.7 copy-start.1
  3.2 0.7 copy-start.2

commit v3 on v2

--- a/solution.py
+++ b/solution.py
@@ -275,7 +275,7 @@
         cost_estimate=pl.CostEstimate(
             flops=14 * length * length * columns, bytes_accessed=22 * length * columns, transcendentals=0
         ),
-    )(fwd_qkv, fwd_segments, parked, bwd_segments, grad_out, loss_tokens)
+    )(*(pltpu.with_memory_space_constraint(x, pltpu.HBM) for x in (fwd_qkv, fwd_segments, parked, bwd_segments, grad_out)), loss_tokens)
     return received, grads
 
 

time: 105 us -> 102 us (0.971)
  local copies, waits for them, and re-layouts: 5.21 us -> 2.64 us
    unnamed x8 -> x2, local copies, waits for them, and re-layouts: 5.21 us -> 2.64 us
where the time goes in v3:
time: 102 us
  Pallas kernels  98.3 us (96%)
  local copies, waits for them, and re-layouts  2.64 us (3%)
  between operations  1.29 us (1%)
    pallas_call x1, Pallas kernels, on_device(): pl.pallas_call(functools.partial(kernel, sections, tensors, replicas), ou...  98.3 us
    unnamed x2, local copies, waits for them, and re-layouts  2.64 us

profile of v3, /device:TPU:0, one launch (start us, length us, event | category | flops | bytes accessed | tf_op | source)
XLA Modules:
  0.0 102.2 jit_solution(6577071064417458226)
XLA Ops:
  1.3 98.3 %shard_map.77 = (bf16[1,256,2048]{2,1,0:T(8,128)(2,1)S(1)}, bf16[3,1,256,2048]{3,2,1,0:T(8,128)(2,1)S(1)}) custom-call(bf16[3,1,256,2048]{3,2,1,0:T(8,128)(2,1)} %fwd_hbm.1, s32[1,256]{1,0:T(1,128)} %fwd_seg_hbm.1, bf16[3,1,64,8192]{3,2,1,0:T(8,128)(2,1)} %parked_hbm.1, s32[1,256]{1,0:T(1,128)} %bwd_seg_hbm.1, bf16[1,256,2048]{2,1,0:T(8,128)(2,1)} %up_hbm.1, ...), custom_call_target="tpu_custom_call" | custom-call | flops 1879048192 | bytes 11534336 | tf_op jit(solution)/shard_map/pallas_call | solution.py:246
  99.6 1.0 copy.11
  100.5 1.7 %copy.12 = bf16[3,1,256,2048]{3,2,1,0:T(8,128)(2,1)} copy(bf16[3,1,256,2048]{3,2,1,0:T(8,128)(2,1)S(1)} %get-tuple-element.5) | data formatting | bytes 6291456

commit v4 on v3

--- a/solution.py
+++ b/solution.py
@@ -232,6 +232,16 @@
     @pl.loop(0, groups)
     def _(g):
         send_grads(g).wait()
+
+
+def store(received, grads, received_out, grads_out, sems):
+    copies = [pltpu.make_async_copy(received, received_out, sems.at[0])]
+    for k in range(3):
+        copies.append(pltpu.make_async_copy(grads.at[k], grads_out.at[k], sems.at[1 + k]))
+    for copy in copies:
+        copy.start()
+    for copy in copies:
+        copy.wait()
 
 
 def on_device(fwd_qkv, fwd_segments, parked, bwd_segments, grad_out, loss_tokens):
@@ -276,7 +286,16 @@
             flops=14 * length * length * columns, bytes_accessed=22 * length * columns, transcendentals=0
         ),
     )(*(pltpu.with_memory_space_constraint(x, pltpu.HBM) for x in (fwd_qkv, fwd_segments, parked, bwd_segments, grad_out)), loss_tokens)
-    return received, grads
+    return pl.pallas_call(
+        store,
+        out_shape=(
+            jax.ShapeDtypeStruct(received.shape, jnp.bfloat16),
+            jax.ShapeDtypeStruct(grads.shape, jnp.bfloat16),
+        ),
+        in_specs=[pl.BlockSpec(memory_space=pl.ANY)] * 2,
+        out_specs=(pl.BlockSpec(memory_space=pl.ANY), pl.BlockSpec(memory_space=pl.ANY)),
+        scratch_shapes=[dma((4,))],
+    )(received, grads)
 
 
 def solution(mesh):

time: 102 us -> 231 us (2.26)
  Pallas kernels: 98.3 us -> 226 us
    pallas_call x0 -> x1, Pallas kernels: none -> 128 us  [on_device(): pl.pallas_call(store, out_shape=(jax.ShapeDtypeStruct(received.shape, jnp...]
where the time goes in v4:
time: 231 us; the launch traced here: 230 us
  Pallas kernels  226 us (98%)
  local copies, waits for them, and re-layouts  2.62 us (1%)
    pallas_call x1, Pallas kernels, on_device(): pl.pallas_call(store, out_shape=(jax.ShapeDtypeStruct(received.shape, jnp...  128 us
    pallas_call x1, Pallas kernels, on_device(): pl.pallas_call(functools.partial(kernel, sections, tensors, replicas), ou...  98.3 us

profile of v4, /device:TPU:0, one launch (start us, length us, event | category | flops | bytes accessed | tf_op | source)
XLA Modules:
  0.0 230.4 jit_solution(7788790074178845475)
XLA Ops:
  1.3 98.3 %shard_map.77 = (bf16[1,256,2048]{2,1,0:T(8,128)(2,1)S(1)}, bf16[3,1,256,2048]{3,2,1,0:T(8,128)(2,1)S(1)}) custom-call(bf16[3,1,256,2048]{3,2,1,0:T(8,128)(2,1)} %fwd_hbm.1, s32[1,256]{1,0:T(1,128)} %fwd_seg_hbm.1, bf16[3,1,64,8192]{3,2,1,0:T(8,128)(2,1)} %parked_hbm.1, s32[1,256]{1,0:T(1,128)} %bwd_seg_hbm.1, bf16[1,256,2048]{2,1,0:T(8,128)(2,1)} %up_hbm.1, ...), custom_call_target="tpu_custom_call" | custom-call | flops 1879048192 | bytes 11534336 | tf_op jit(solution)/shard_map/pallas_call | solution.py:256
  99.6 0.0 copy-start
  99.6 1.6 copy-done
  101.2 0.0 copy-start.1
  101.2 1.0 copy-done.1
  102.2 128.2 %shard_map.78 = (bf16[1,256,2048]{2,1,0:T(8,128)(2,1)}, bf16[3,1,256,2048]{3,2,1,0:T(8,128)(2,1)}) custom-call(bf16[1,256,2048]{2,1,0:T(8,128)(2,1)} %copy-done.1, bf16[3,1,256,2048]{3,2,1,0:T(8,128)(2,1)} %copy-done), custom_call_target="tpu_custom_call" | custom-call | tf_op jit(solution)/shard_map/pallas_call | solution.py:289
Async XLA Ops:
  99.6 1.7 copy-start
  101.2 1.0 copy-start.1

commit v5 on v4

--- a/solution.py
+++ b/solution.py
@@ -50,6 +50,19 @@
     columns = fwd.shape[2]
     groups = columns // width
     rows = parked_hbm.shape[2]
+    heads = columns // HEAD_DIM
+
+    def head_span(h):
+        return pl.ds(pl.multiple_of(h * HEAD_DIM, HEAD_DIM), HEAD_DIM)
+
+    def load_fwd(h):
+        cols = head_span(h)
+        return pltpu.make_async_copy(fwd_hbm.at[:, 0, :, cols], fwd.at[:, :, cols], fwd_sem.at[h])
+
+    seg_copy = pltpu.make_async_copy(fwd_seg_hbm, fwd_seg, small_sem.at[0])
+    tok_copy = pltpu.make_async_copy(tokens_hbm, tokens, small_sem.at[1])
+    seg_copy.start()
+    load_fwd(0).start()
 
     barrier = pltpu.get_barrier_semaphore()
     greeted = 0
@@ -67,9 +80,6 @@
     def span(g):
         return pl.ds(pl.multiple_of(g * width, width), width)
 
-    def load_fwd(g):
-        return pltpu.make_async_copy(fwd_hbm.at[:, 0, :, span(g)], fwd.at[:, :, span(g)], fwd_sem.at[g])
-
     def load_up(g):
         return pltpu.make_async_copy(up_hbm.at[0, :, span(g)], up.at[:, span(g)], up_sem.at[g])
 
@@ -106,12 +116,12 @@
             device_id_type=MESH,
         )
 
-    def send_out(g):
-        return pltpu.make_async_remote_copy(
-            src_ref=out.at[:, span(g)],
-            dst_ref=received_hbm.at[0, :, span(g)],
-            send_sem=out_send.at[g],
-            recv_sem=out_recv.at[g],
+    def send_out(h):
+        return pltpu.make_async_remote_copy(
+            src_ref=out.at[:, head_span(h)],
+            dst_ref=received_hbm.at[0, :, head_span(h)],
+            send_sem=out_send.at[h],
+            recv_sem=out_recv.at[h],
             device_id={"pipe": after},
             device_id_type=MESH,
         )
@@ -145,28 +155,20 @@
         device_id_type=MESH,
     )
 
-    seg_copy = pltpu.make_async_copy(fwd_seg_hbm, fwd_seg, small_sem.at[0])
-    tok_copy = pltpu.make_async_copy(tokens_hbm, tokens, small_sem.at[1])
-    seg_copy.start()
+    def forward(h):
+        load_fwd(h).wait()
+        cols = head_span(h)
+        probs = softmax(fwd[0, :, cols], fwd[1, :, cols], fwd_bias[...])
+        mixed = dot(probs.astype(jnp.bfloat16), fwd[2, :, cols], ((1,), (0,)))
+        out[:, cols] = mixed.astype(jnp.bfloat16)
+
     tok_copy.start()
-    pl.loop(0, groups)(lambda g: load_fwd(g).start())
-    pl.loop(0, groups)(lambda g: load_own(g).start())
-    pl.loop(0, groups)(lambda g: load_up(g).start())
-
-    def forward(g):
-        load_fwd(g).wait()
-        for h in range(GROUP):
-            cols = pl.ds(pl.multiple_of(g * width + h * HEAD_DIM, HEAD_DIM), HEAD_DIM)
-            probs = softmax(fwd[0, :, cols], fwd[1, :, cols], fwd_bias[...])
-            mixed = dot(probs.astype(jnp.bfloat16), fwd[2, :, cols], ((1,), (0,)))
-            out[:, cols] = mixed.astype(jnp.bfloat16)
-
-    tok_copy.wait()
-    token_tile[...] = jnp.full(token_tile.shape, tokens[0], jnp.int32)
-
+    pl.loop(1, heads)(lambda h: load_fwd(h).start())
     seg_copy.wait()
     fwd_bias[...] = mask_bias(fwd_seg[...])
     forward(0)
+    tok_copy.wait()
+    token_tile[...] = jnp.full(token_tile.shape, tokens[0], jnp.int32)
 
     pl.semaphore_wait(barrier, greeted)
     send_out(0).start()
@@ -180,11 +182,13 @@
 
     for g in range(AHEAD):
         exchange(g)
-
-    @pl.loop(1, groups)
-    def _(g):
-        forward(g)
-        send_out(g).start()
+    pl.loop(0, groups)(lambda g: load_own(g).start())
+    pl.loop(0, groups)(lambda g: load_up(g).start())
+
+    @pl.loop(1, heads)
+    def _(h):
+        forward(h)
+        send_out(h).start()
 
     send_segment.wait()
     bwd_bias[...] = mask_bias(bwd_seg[...])
@@ -227,7 +231,8 @@
     def _(g):
         for step in range(1, tensors):
             send_part(step, g).wait_send()
-        send_out(g).wait()
+
+    pl.loop(0, heads)(lambda h: send_out(h).wait())
 
     @pl.loop(0, groups)
     def _(g):
@@ -249,7 +254,8 @@
     tensors = lax.axis_size("tensor")
     replicas = lax.axis_size("dp")
     length, columns = fwd_qkv.shape[2], fwd_qkv.shape[3]
-    groups = columns // (GROUP * HEAD_DIM)
+    heads = columns // HEAD_DIM
+    groups = heads // GROUP
     if sections > 2:
         grad_out = lax.ppermute(grad_out, "pipe", [(i, (-i) % sections) for i in range(sections)])
     dma = pltpu.SemaphoreType.DMA
@@ -274,9 +280,9 @@
             pltpu.SMEM((1,), jnp.int32),
             pltpu.VMEM((8, HEAD_DIM), jnp.int32),
             pltpu.VMEM((replicas, 8, HEAD_DIM), jnp.int32),
-            dma((groups,)), dma((groups,)), dma((groups,)), dma((2,)),
+            dma((heads,)), dma((groups,)), dma((groups,)), dma((2,)),
             dma((tensors - 1, groups)), dma((tensors - 1, groups)),
-            dma((groups,)), dma((groups,)), dma((groups,)), dma((groups,)),
+            dma((heads,)), dma((heads,)), dma((groups,)), dma((groups,)),
             dma, dma, dma((replicas,)), dma((replicas,)),
         ],
         compiler_params=pltpu.CompilerParams(
@@ -295,6 +301,7 @@
         in_specs=[pl.BlockSpec(memory_space=pl.ANY)] * 2,
         out_specs=(pl.BlockSpec(memory_space=pl.ANY), pl.BlockSpec(memory_space=pl.ANY)),
         scratch_shapes=[dma((4,))],
+        compiler_params=pltpu.CompilerParams(vmem_limit_bytes=1024 * 1024),
     )(received, grads)
 
 

time: 231 us -> 102 us (0.44)
  Pallas kernels: 226 us -> 101 us
  local copies, waits for them, and re-layouts: 2.62 us -> 0 us
    pallas_call x1, Pallas kernels: 128 us -> 2.04 us  [on_device(): pl.pallas_call(store, out_shape=(jax.ShapeDtypeStruct(received.shape, jnp...]
    unnamed x4 -> x0, local copies, waits for them, and re-layouts: 2.62 us -> none
where the time goes in v5:
time: 102 us
  Pallas kernels  101 us (99%)
  between operations  1.29 us (1%)
    pallas_call x1, Pallas kernels, on_device(): pl.pallas_call(functools.partial(kernel, sections, tensors, replicas), ou...  98.5 us
    pallas_call x1, Pallas kernels, on_device(): pl.pallas_call(store, out_shape=(jax.ShapeDtypeStruct(received.shape, jnp...  2.04 us

profile of v5, /device:TPU:0, one launch (start us, length us, event | category | flops | bytes accessed | tf_op | source)
XLA Modules:
  0.0 101.8 jit_solution(5403417058092321532)
XLA Ops:
  1.3 98.5 %shard_map.77 = (bf16[1,256,2048]{2,1,0:T(8,128)(2,1)S(1)}, bf16[3,1,256,2048]{3,2,1,0:T(8,128)(2,1)S(1)}) custom-call(bf16[3,1,256,2048]{3,2,1,0:T(8,128)(2,1)} %fwd_hbm.1, s32[1,256]{1,0:T(1,128)} %fwd_seg_hbm.1, bf16[3,1,64,8192]{3,2,1,0:T(8,128)(2,1)} %parked_hbm.1, s32[1,256]{1,0:T(1,128)} %bwd_seg_hbm.1, bf16[1,256,2048]{2,1,0:T(8,128)(2,1)} %up_hbm.1, ...), custom_call_target="tpu_custom_call" | custom-call | flops 1879048192 | bytes 11534336 | tf_op jit(solution)/shard_map/pallas_call | solution.py:262
  99.8 2.0 %shard_map.78 = (bf16[1,256,2048]{2,1,0:T(8,128)(2,1)}, bf16[3,1,256,2048]{3,2,1,0:T(8,128)(2,1)}) custom-call(bf16[1,256,2048]{2,1,0:T(8,128)(2,1)S(1)} %get-tuple-element.4.received, bf16[3,1,256,2048]{3,2,1,0:T(8,128)(2,1)S(1)} %get-tuple-element.5.grads), custom_call_target="tpu_custom_call" | custom-call | tf_op jit(solution)/shard_map/pallas_call | solution.py:295

commit v6 on v5

--- a/solution.py
+++ b/solution.py
@@ -33,7 +33,7 @@
 def kernel(
     sections, tensors, replicas,
     fwd_hbm, fwd_seg_hbm, parked_hbm, bwd_seg_hbm, up_hbm, tokens_hbm,
-    received_hbm, grads_hbm,
+    landed_out, landed_grads,
     fwd, out, stash, up, grads, fwd_bias, bwd_bias, fwd_seg, bwd_seg, tokens, token_tile, token_all,
     fwd_sem, up_sem, own_sem, small_sem,
     part_send, part_recv, out_send, out_recv, grad_send, grad_recv,
@@ -118,8 +118,8 @@
 
     def send_out(h):
         return pltpu.make_async_remote_copy(
-            src_ref=out.at[:, head_span(h)],
-            dst_ref=received_hbm.at[0, :, head_span(h)],
+            src_ref=out.at[h],
+            dst_ref=landed_out.at[h],
             send_sem=out_send.at[h],
             recv_sem=out_recv.at[h],
             device_id={"pipe": after},
@@ -128,8 +128,8 @@
 
     def send_grads(g):
         return pltpu.make_async_remote_copy(
-            src_ref=grads.at[:, :, span(g)],
-            dst_ref=grads_hbm.at[:, 0, :, span(g)],
+            src_ref=grads.at[g],
+            dst_ref=landed_grads.at[g],
             send_sem=grad_send.at[g],
             recv_sem=grad_recv.at[g],
             device_id={"pipe": mirror},
@@ -160,7 +160,7 @@
         cols = head_span(h)
         probs = softmax(fwd[0, :, cols], fwd[1, :, cols], fwd_bias[...])
         mixed = dot(probs.astype(jnp.bfloat16), fwd[2, :, cols], ((1,), (0,)))
-        out[:, cols] = mixed.astype(jnp.bfloat16)
+        out[h] = mixed.astype(jnp.bfloat16)
 
     tok_copy.start()
     pl.loop(1, heads)(lambda h: load_fwd(h).start())
@@ -219,9 +219,10 @@
             grad_logits = (probs * (grad_probs - center) * SCALE).astype(jnp.bfloat16)
             grad_query = dot(grad_logits, key, ((1,), (0,)))
             grad_key = dot(grad_logits, query, ((0,), (0,)))
-            grads[0, :, cols] = (grad_query * factor).astype(jnp.bfloat16)
-            grads[1, :, cols] = (grad_key * factor).astype(jnp.bfloat16)
-            grads[2, :, cols] = (grad_value * factor).astype(jnp.bfloat16)
+            place = slice(h * HEAD_DIM, (h + 1) * HEAD_DIM)
+            grads[g, 0, :, place] = (grad_query * factor).astype(jnp.bfloat16)
+            grads[g, 1, :, place] = (grad_key * factor).astype(jnp.bfloat16)
+            grads[g, 2, :, place] = (grad_value * factor).astype(jnp.bfloat16)
         send_grads(g).start()
 
     for other in range(replicas):
@@ -239,10 +240,19 @@
         send_grads(g).wait()
 
 
-def store(received, grads, received_out, grads_out, sems):
-    copies = [pltpu.make_async_copy(received, received_out, sems.at[0])]
-    for k in range(3):
-        copies.append(pltpu.make_async_copy(grads.at[k], grads_out.at[k], sems.at[1 + k]))
+def store(landed_out, landed_grads, received, grads, out_sem, grad_sem):
+    heads, groups = landed_out.shape[0], landed_grads.shape[0]
+    width = GROUP * HEAD_DIM
+
+    def store_out(h):
+        cols = pl.ds(h * HEAD_DIM, HEAD_DIM)
+        return pltpu.make_async_copy(landed_out.at[h], received.at[0, :, cols], out_sem.at[h])
+
+    def store_grads(g):
+        cols = pl.ds(g * width, width)
+        return pltpu.make_async_copy(landed_grads.at[g], grads.at[:, 0, :, cols], grad_sem.at[g])
+
+    copies = [store_grads(g) for g in range(groups)] + [store_out(h) for h in range(heads)]
     for copy in copies:
         copy.start()
     for copy in copies:
@@ -259,20 +269,20 @@
     if sections > 2:
         grad_out = lax.ppermute(grad_out, "pipe", [(i, (-i) % sections) for i in range(sections)])
     dma = pltpu.SemaphoreType.DMA
-    received, grads = pl.pallas_call(
+    landed_out, landed_grads = pl.pallas_call(
         functools.partial(kernel, sections, tensors, replicas),
         out_shape=(
-            jax.ShapeDtypeStruct((1, length, columns), jnp.bfloat16),
-            jax.ShapeDtypeStruct((3, 1, length, columns), jnp.bfloat16),
+            jax.ShapeDtypeStruct((heads, length, HEAD_DIM), jnp.bfloat16),
+            jax.ShapeDtypeStruct((groups, 3, length, GROUP * HEAD_DIM), jnp.bfloat16),
         ),
         in_specs=[pl.BlockSpec(memory_space=pltpu.HBM)] * 6,
         out_specs=(pl.BlockSpec(memory_space=pl.ANY), pl.BlockSpec(memory_space=pl.ANY)),
         scratch_shapes=[
             pltpu.VMEM((3, length, columns), jnp.bfloat16),
-            pltpu.VMEM((length, columns), jnp.bfloat16),
+            pltpu.VMEM((heads, length, HEAD_DIM), jnp.bfloat16),
             pltpu.VMEM((3, length, columns), jnp.bfloat16),
             pltpu.VMEM((length, columns), jnp.bfloat16),
-            pltpu.VMEM((3, length, columns), jnp.bfloat16),
+            pltpu.VMEM((groups, 3, length, GROUP * HEAD_DIM), jnp.bfloat16),
             pltpu.VMEM((length, length), jnp.float32),
             pltpu.VMEM((length, length), jnp.float32),
             pltpu.VMEM((1, length), jnp.int32),
@@ -295,14 +305,14 @@
     return pl.pallas_call(
         store,
         out_shape=(
-            jax.ShapeDtypeStruct(received.shape, jnp.bfloat16),
-            jax.ShapeDtypeStruct(grads.shape, jnp.bfloat16),
+            jax.ShapeDtypeStruct((1, length, columns), jnp.bfloat16),
+            jax.ShapeDtypeStruct((3, 1, length, columns), jnp.bfloat16),
         ),
         in_specs=[pl.BlockSpec(memory_space=pl.ANY)] * 2,
         out_specs=(pl.BlockSpec(memory_space=pl.ANY), pl.BlockSpec(memory_space=pl.ANY)),
-        scratch_shapes=[dma((4,))],
+        scratch_shapes=[dma((heads,)), dma((groups,))],
         compiler_params=pltpu.CompilerParams(vmem_limit_bytes=1024 * 1024),
-    )(received, grads)
+    )(landed_out, landed_grads)
 
 
 def solution(mesh):

time: 102 us -> 102 us (level)
  no operation moved by 1% of the time
where the time goes in v6:
time: 102 us
  Pallas kernels  101 us (99%)
  between operations  1.29 us (1%)
    pallas_call x1, Pallas kernels, on_device(): pl.pallas_call(functools.partial(kernel, sections, tensors, replicas), ou...  98.5 us
    pallas_call x1, Pallas kernels, on_device(): pl.pallas_call(store, out_shape=(jax.ShapeDtypeStruct((1, length, columns...  2.21 us

profile of v6, /device:TPU:0, one launch (start us, length us, event | category | flops | bytes accessed | tf_op | source)
XLA Modules:
  0.0 102.0 jit_solution(16445712747007003849)
XLA Ops:
  1.3 98.5 %shard_map.77 = (bf16[16,256,128]{2,1,0:T(8,128)(2,1)S(1)}, bf16[8,3,256,256]{3,2,1,0:T(8,128)(2,1)S(1)}) custom-call(bf16[3,1,256,2048]{3,2,1,0:T(8,128)(2,1)} %fwd_hbm.1, s32[1,256]{1,0:T(1,128)} %fwd_seg_hbm.1, bf16[3,1,64,8192]{3,2,1,0:T(8,128)(2,1)} %parked_hbm.1, s32[1,256]{1,0:T(1,128)} %bwd_seg_hbm.1, bf16[1,256,2048]{2,1,0:T(8,128)(2,1)} %up_hbm.1, ...), custom_call_target="tpu_custom_call" | custom-call | flops 1879048192 | bytes 11534336 | tf_op jit(solution)/shard_map/pallas_call | solution.py:272
  99.8 2.2 %shard_map.78 = (bf16[1,256,2048]{2,1,0:T(8,128)(2,1)}, bf16[3,1,256,2048]{3,2,1,0:T(8,128)(2,1)}) custom-call(bf16[16,256,128]{2,1,0:T(8,128)(2,1)S(1)} %get-tuple-element.4.landed_out, bf16[8,3,256,256]{3,2,1,0:T(8,128)(2,1)S(1)} %get-tuple-element.5.landed_grads), custom_call_target="tpu_custom_call" | custom-call | tf_op jit(solution)/shard_map/pallas_call | solution.py:305

commit v7 on v5

--- a/solution.py
+++ b/solution.py
@@ -11,6 +11,7 @@
 SCALE = HEAD_DIM ** (-0.5)
 GROUP = 2
 AHEAD = 2
+SPREAD_AT, TOTAL_AT = 2, 6
 MESH = pl.DeviceIdType.MESH
 
 
@@ -34,10 +35,11 @@
     sections, tensors, replicas,
     fwd_hbm, fwd_seg_hbm, parked_hbm, bwd_seg_hbm, up_hbm, tokens_hbm,
     received_hbm, grads_hbm,
-    fwd, out, stash, up, grads, fwd_bias, bwd_bias, fwd_seg, bwd_seg, tokens, token_tile, token_all,
+    fwd, out, stash, up, grads, fwd_bias, bwd_bias, fwd_seg, bwd_seg, tokens,
+    token_tile, token_got, token_all, token_total,
     fwd_sem, up_sem, own_sem, small_sem,
     part_send, part_recv, out_send, out_recv, grad_send, grad_recv,
-    seg_send, seg_recv, tok_send, tok_recv,
+    seg_send, seg_recv, tok_send, tok_recv, spread_send, spread_recv, total_send, total_recv,
 ):
     section = lax.axis_index("pipe")
     lane = lax.axis_index("tensor")
@@ -69,13 +71,22 @@
     for step in range(1, tensors):
         pl.semaphore_signal(barrier, inc=1, device_id={"tensor": lax.rem(lane + step, tensors)}, device_id_type=MESH)
         greeted += 1
-    for other in range(replicas):
-        pl.semaphore_signal(barrier, inc=1, device_id={"pipe": mirror, "dp": other}, device_id_type=MESH)
-        greeted += 1
+    pl.semaphore_signal(barrier, inc=1, device_id={"pipe": mirror}, device_id_type=MESH)
+    greeted += 1
     if sections > 2:
         for other in (after, before):
             pl.semaphore_signal(barrier, inc=1, device_id={"pipe": other}, device_id_type=MESH)
             greeted += 1
+
+    relays = lane == tensors - 1
+
+    def other_replica(step):
+        return lax.rem(replica + step, replicas)
+
+    @pl.when(relays)
+    def _():
+        for step in range(1, replicas):
+            pl.semaphore_signal(barrier, inc=1, device_id={"dp": other_replica(step)}, device_id_type=MESH)
 
     def span(g):
         return pl.ds(pl.multiple_of(g * width, width), width)
@@ -136,13 +147,32 @@
             device_id_type=MESH,
         )
 
-    def send_tokens(other, mine):
-        return pltpu.make_async_remote_copy(
-            src_ref=token_tile,
-            dst_ref=token_all.at[mine],
-            send_sem=tok_send.at[other],
-            recv_sem=tok_recv.at[mine],
-            device_id={"pipe": mirror, "dp": other},
+    send_tokens = pltpu.make_async_remote_copy(
+        src_ref=token_tile,
+        dst_ref=token_got,
+        send_sem=tok_send,
+        recv_sem=tok_recv,
+        device_id={"pipe": mirror},
+        device_id_type=MESH,
+    )
+
+    def spread_tokens(step):
+        return pltpu.make_async_remote_copy(
+            src_ref=token_got,
+            dst_ref=token_all.at[step - 1],
+            send_sem=spread_send.at[step - 1],
+            recv_sem=spread_recv.at[step - 1],
+            device_id={"dp": other_replica(step)},
+            device_id_type=MESH,
+        )
+
+    def hand_total(step):
+        return pltpu.make_async_remote_copy(
+            src_ref=token_total,
+            dst_ref=token_total,
+            send_sem=total_send.at[step - 1],
+            recv_sem=total_recv,
+            device_id={"tensor": lax.rem(lane + step, tensors)},
             device_id_type=MESH,
         )
 
@@ -170,11 +200,17 @@
     tok_copy.wait()
     token_tile[...] = jnp.full(token_tile.shape, tokens[0], jnp.int32)
 
-    pl.semaphore_wait(barrier, greeted)
+    @pl.when(relays)
+    def _():
+        pl.semaphore_wait(barrier, greeted + replicas - 1)
+        send_tokens.start()
+
+    @pl.when(lane != tensors - 1)
+    def _():
+        pl.semaphore_wait(barrier, greeted)
+
+    send_segment.start()
     send_out(0).start()
-    send_segment.start()
-    for other in range(replicas):
-        send_tokens(other, replica).start()
 
     def exchange(g):
         for step in range(1, tensors):
@@ -190,13 +226,30 @@
         forward(h)
         send_out(h).start()
 
+        @pl.when(relays & (h == SPREAD_AT))
+        def _():
+            send_tokens.wait()
+            for step in range(1, replicas):
+                spread_tokens(step).start()
+
+        @pl.when(relays & (h == TOTAL_AT))
+        def _():
+            total = token_got[...]
+            for step in range(1, replicas):
+                spread_tokens(step).wait()
+                total += token_all[step - 1]
+            token_total[...] = total
+            for step in range(1, tensors):
+                hand_total(step).start()
+
     send_segment.wait()
     bwd_bias[...] = mask_bias(bwd_seg[...])
-    total = jnp.zeros((1, HEAD_DIM), jnp.float32)
-    for other in range(replicas):
-        send_tokens(other, other).wait_recv()
-        total += token_all[other, 0:1, :].astype(jnp.float32)
-    factor = jnp.float32(replicas * length) / total
+
+    @pl.when(lane != tensors - 1)
+    def _():
+        hand_total(1).wait_recv()
+
+    factor = jnp.float32(replicas * length) / token_total[0:1, :].astype(jnp.float32)
 
     @pl.loop(0, groups)
     def _(g):
@@ -224,8 +277,10 @@
             grads[2, :, cols] = (grad_value * factor).astype(jnp.bfloat16)
         send_grads(g).start()
 
-    for other in range(replicas):
-        send_tokens(other, replica).wait_send()
+    @pl.when(relays)
+    def _():
+        for step in range(1, tensors):
+            hand_total(step).wait_send()
 
     @pl.loop(0, groups)
     def _(g):
@@ -279,11 +334,13 @@
             pltpu.VMEM((1, length), jnp.int32),
             pltpu.SMEM((1,), jnp.int32),
             pltpu.VMEM((8, HEAD_DIM), jnp.int32),
-            pltpu.VMEM((replicas, 8, HEAD_DIM), jnp.int32),
+            pltpu.VMEM((8, HEAD_DIM), jnp.int32),
+            pltpu.VMEM((replicas - 1, 8, HEAD_DIM), jnp.int32),
+            pltpu.VMEM((8, HEAD_DIM), jnp.int32),
             dma((heads,)), dma((groups,)), dma((groups,)), dma((2,)),
             dma((tensors - 1, groups)), dma((tensors - 1, groups)),
             dma((heads,)), dma((heads,)), dma((groups,)), dma((groups,)),
-            dma, dma, dma((replicas,)), dma((replicas,)),
+            dma, dma, dma, dma, dma((replicas - 1,)), dma((replicas - 1,)), dma((tensors - 1,)), dma,
         ],
         compiler_params=pltpu.CompilerParams(
             collective_id=0, has_side_effects=True, vmem_limit_bytes=48 * 1024 * 1024

time: 102 us -> 100 us (0.980)
  Pallas kernels: 101 us -> 99 us
    pallas_call x1, Pallas kernels: 98.5 us -> 96.9 us  [on_device(): pl.pallas_call(functools.partial(kernel, sections, tensors, replicas), ou...]
where the time goes in v7:
time: 100 us
  Pallas kernels  99 us (99%)
  between operations  1.29 us (1%)
    pallas_call x1, Pallas kernels, on_device(): pl.pallas_call(functools.partial(kernel, sections, tensors, replicas), ou...  96.9 us
    pallas_call x1, Pallas kernels, on_device(): pl.pallas_call(store, out_shape=(jax.ShapeDtypeStruct(received.shape, jnp...  2.04 us

profile of v7, /device:TPU:0, one launch (start us, length us, event | category | flops | bytes accessed | tf_op | source)
XLA Modules:
  0.0 100.2 jit_solution(17138247778860742889)
XLA Ops:
  1.3 96.9 %shard_map.77 = (bf16[1,256,2048]{2,1,0:T(8,128)(2,1)S(1)}, bf16[3,1,256,2048]{3,2,1,0:T(8,128)(2,1)S(1)}) custom-call(bf16[3,1,256,2048]{3,2,1,0:T(8,128)(2,1)} %fwd_hbm.1, s32[1,256]{1,0:T(1,128)} %fwd_seg_hbm.1, bf16[3,1,64,8192]{3,2,1,0:T(8,128)(2,1)} %parked_hbm.1, s32[1,256]{1,0:T(1,128)} %bwd_seg_hbm.1, bf16[1,256,2048]{2,1,0:T(8,128)(2,1)} %up_hbm.1, ...), custom_call_target="tpu_custom_call" | custom-call | flops 1879048192 | bytes 11534336 | tf_op jit(solution)/shard_map/pallas_call | solution.py:317
  98.2 2.0 %shard_map.78 = (bf16[1,256,2048]{2,1,0:T(8,128)(2,1)}, bf16[3,1,256,2048]{3,2,1,0:T(8,128)(2,1)}) custom-call(bf16[1,256,2048]{2,1,0:T(8,128)(2,1)S(1)} %get-tuple-element.4.received, bf16[3,1,256,2048]{3,2,1,0:T(8,128)(2,1)S(1)} %get-tuple-element.5.grads), custom_call_target="tpu_custom_call" | custom-call | tf_op jit(solution)/shard_map/pallas_call | solution.py:352

commit v8 on v7

--- a/solution.py
+++ b/solution.py
@@ -11,7 +11,8 @@
 SCALE = HEAD_DIM ** (-0.5)
 GROUP = 2
 AHEAD = 2
-SPREAD_AT, TOTAL_AT = 2, 6
+SPREAD_AT, TOTAL_AT = 2, 5
+FIRST = 6
 MESH = pl.DeviceIdType.MESH
 
 
@@ -22,7 +23,7 @@
 def softmax(query, key, bias):
     logits = dot(query, key, ((1,), (1,))) * SCALE + bias
     weights = jnp.exp(logits - jnp.max(logits, axis=-1, keepdims=True))
-    return weights / jnp.sum(weights, axis=-1, keepdims=True)
+    return weights * (1.0 / jnp.sum(weights, axis=-1, keepdims=True))
 
 
 def mask_bias(segment):
@@ -221,7 +222,7 @@
     pl.loop(0, groups)(lambda g: load_own(g).start())
     pl.loop(0, groups)(lambda g: load_up(g).start())
 
-    @pl.loop(1, heads)
+    @pl.loop(1, FIRST)
     def _(h):
         forward(h)
         send_out(h).start()
@@ -276,6 +277,12 @@
             grads[1, :, cols] = (grad_key * factor).astype(jnp.bfloat16)
             grads[2, :, cols] = (grad_value * factor).astype(jnp.bfloat16)
         send_grads(g).start()
+
+        @pl.when(FIRST + GROUP * g < heads)
+        def _():
+            for h in range(GROUP):
+                forward(FIRST + GROUP * g + h)
+                send_out(FIRST + GROUP * g + h).start()
 
     @pl.when(relays)
     def _():

time: 100 us -> 106 us (1.060)
  Pallas kernels: 99 us -> 105 us
    pallas_call x1, Pallas kernels: 96.9 us -> 103 us  [on_device(): pl.pallas_call(functools.partial(kernel, sections, tensors, replicas), ou...]
where the time goes in v8:
time: 106 us
  Pallas kernels  105 us (99%)
  between operations  1.29 us (1%)
    pallas_call x1, Pallas kernels, on_device(): pl.pallas_call(functools.partial(kernel, sections, tensors, replicas), ou...  103 us

profile of v8, /device:TPU:0, one launch (start us, length us, event | category | flops | bytes accessed | tf_op | source)
XLA Modules:
  0.0 105.8 jit_solution(1022414478164101686)
XLA Ops:
  1.3 102.5 %shard_map.77 = (bf16[1,256,2048]{2,1,0:T(8,128)(2,1)S(1)}, bf16[3,1,256,2048]{3,2,1,0:T(8,128)(2,1)S(1)}) custom-call(bf16[3,1,256,2048]{3,2,1,0:T(8,128)(2,1)} %fwd_hbm.1, s32[1,256]{1,0:T(1,128)} %fwd_seg_hbm.1, bf16[3,1,64,8192]{3,2,1,0:T(8,128)(2,1)} %parked_hbm.1, s32[1,256]{1,0:T(1,128)} %bwd_seg_hbm.1, bf16[1,256,2048]{2,1,0:T(8,128)(2,1)} %up_hbm.1, ...), custom_call_target="tpu_custom_call" | custom-call | flops 1879048192 | bytes 11534336 | tf_op jit(solution)/shard_map/pallas_call | solution.py:324
  103.8 2.0 %shard_map.78 = (bf16[1,256,2048]{2,1,0:T(8,128)(2,1)}, bf16[3,1,256,2048]{3,2,1,0:T(8,128)(2,1)}) custom-call(bf16[1,256,2048]{2,1,0:T(8,128)(2,1)S(1)} %get-tuple-element.4.received, bf16[3,1,256,2048]{3,2,1,0:T(8,128)(2,1)S(1)} %get-tuple-element.5.grads), custom_call_target="tpu_custom_call" | custom-call | tf_op jit(solution)/shard_map/pallas_call | solution.py:359

commit v9 on v7

--- a/solution.py
+++ b/solution.py
@@ -22,7 +22,7 @@
 def softmax(query, key, bias):
     logits = dot(query, key, ((1,), (1,))) * SCALE + bias
     weights = jnp.exp(logits - jnp.max(logits, axis=-1, keepdims=True))
-    return weights / jnp.sum(weights, axis=-1, keepdims=True)
+    return weights * (1.0 / jnp.sum(weights, axis=-1, keepdims=True))
 
 
 def mask_bias(segment):
@@ -65,6 +65,8 @@
     tok_copy = pltpu.make_async_copy(tokens_hbm, tokens, small_sem.at[1])
     seg_copy.start()
     load_fwd(0).start()
+    tok_copy.start()
+    load_fwd(1).start()
 
     barrier = pltpu.get_barrier_semaphore()
     greeted = 0
@@ -147,6 +149,18 @@
             device_id_type=MESH,
         )
 
+    def send_first(half):
+        part = pl.ds(half * (length // 2), length // 2)
+        place = pl.ds(0, HEAD_DIM)
+        return pltpu.make_async_remote_copy(
+            src_ref=out.at[part, place],
+            dst_ref=received_hbm.at[0, part, place],
+            send_sem=out_send.at[half * heads],
+            recv_sem=out_recv.at[half * heads],
+            device_id={"pipe": after},
+            device_id_type=MESH,
+        )
+
     send_tokens = pltpu.make_async_remote_copy(
         src_ref=token_tile,
         dst_ref=token_got,
@@ -192,25 +206,35 @@
         mixed = dot(probs.astype(jnp.bfloat16), fwd[2, :, cols], ((1,), (0,)))
         out[:, cols] = mixed.astype(jnp.bfloat16)
 
-    tok_copy.start()
-    pl.loop(1, heads)(lambda h: load_fwd(h).start())
+    def first_rows(half):
+        part = slice(half * (length // 2), (half + 1) * (length // 2))
+        probs = softmax(fwd[0, part, :HEAD_DIM], fwd[1, :, :HEAD_DIM], fwd_bias[part, :])
+        mixed = dot(probs.astype(jnp.bfloat16), fwd[2, :, :HEAD_DIM], ((1,), (0,)))
+        out[part, :HEAD_DIM] = mixed.astype(jnp.bfloat16)
+
     seg_copy.wait()
     fwd_bias[...] = mask_bias(fwd_seg[...])
-    forward(0)
+    load_fwd(0).wait()
+    first_rows(0)
+
+    @pl.when(relays)
+    def _():
+        pl.semaphore_wait(barrier, greeted + replicas - 1)
+
+    @pl.when(lane != tensors - 1)
+    def _():
+        pl.semaphore_wait(barrier, greeted)
+
+    send_first(0).start()
+    first_rows(1)
+    send_first(1).start()
+    send_segment.start()
     tok_copy.wait()
     token_tile[...] = jnp.full(token_tile.shape, tokens[0], jnp.int32)
 
     @pl.when(relays)
     def _():
-        pl.semaphore_wait(barrier, greeted + replicas - 1)
         send_tokens.start()
-
-    @pl.when(lane != tensors - 1)
-    def _():
-        pl.semaphore_wait(barrier, greeted)
-
-    send_segment.start()
-    send_out(0).start()
 
     def exchange(g):
         for step in range(1, tensors):
@@ -218,6 +242,7 @@
 
     for g in range(AHEAD):
         exchange(g)
+    pl.loop(2, heads)(lambda h: load_fwd(h).start())
     pl.loop(0, groups)(lambda g: load_own(g).start())
     pl.loop(0, groups)(lambda g: load_up(g).start())
 
@@ -287,7 +312,9 @@
         for step in range(1, tensors):
             send_part(step, g).wait_send()
 
-    pl.loop(0, heads)(lambda h: send_out(h).wait())
+    for half in range(2):
+        send_first(half).wait()
+    pl.loop(1, heads)(lambda h: send_out(h).wait())
 
     @pl.loop(0, groups)
     def _(g):
@@ -339,7 +366,7 @@
             pltpu.VMEM((8, HEAD_DIM), jnp.int32),
             dma((heads,)), dma((groups,)), dma((groups,)), dma((2,)),
             dma((tensors - 1, groups)), dma((tensors - 1, groups)),
-            dma((heads,)), dma((heads,)), dma((groups,)), dma((groups,)),
+            dma((heads + 1,)), dma((heads + 1,)), dma((groups,)), dma((groups,)),
             dma, dma, dma, dma, dma((replicas - 1,)), dma((replicas - 1,)), dma((tensors - 1,)), dma,
         ],
         compiler_params=pltpu.CompilerParams(

time: 100 us -> 100 us (level)
  no operation moved by 1% of the time
where the time goes in v9:
time: 100 us
  Pallas kernels  98.9 us (99%)
  between operations  1.29 us (1%)
    pallas_call x1, Pallas kernels, on_device(): pl.pallas_call(functools.partial(kernel, sections, tensors, replicas), ou...  96.8 us
    pallas_call x1, Pallas kernels, on_device(): pl.pallas_call(store, out_shape=(jax.ShapeDtypeStruct(received.shape, jnp...  2.04 us

profile of v9, /device:TPU:0, one launch (start us, length us, event | category | flops | bytes accessed | tf_op | source)
XLA Modules:
  0.0 100.2 jit_solution(15184197970625735148)
XLA Ops:
  1.3 96.8 %shard_map.77 = (bf16[1,256,2048]{2,1,0:T(8,128)(2,1)S(1)}, bf16[3,1,256,2048]{3,2,1,0:T(8,128)(2,1)S(1)}) custom-call(bf16[3,1,256,2048]{3,2,1,0:T(8,128)(2,1)} %fwd_hbm.1, s32[1,256]{1,0:T(1,128)} %fwd_seg_hbm.1, bf16[3,1,64,8192]{3,2,1,0:T(8,128)(2,1)} %parked_hbm.1, s32[1,256]{1,0:T(1,128)} %bwd_seg_hbm.1, bf16[1,256,2048]{2,1,0:T(8,128)(2,1)} %up_hbm.1, ...), custom_call_target="tpu_custom_call" | custom-call | flops 1879048192 | bytes 11534336 | tf_op jit(solution)/shard_map/pallas_call | solution.py:344
  98.1 2.0 %shard_map.78 = (bf16[1,256,2048]{2,1,0:T(8,128)(2,1)}, bf16[3,1,256,2048]{3,2,1,0:T(8,128)(2,1)}) custom-call(bf16[1,256,2048]{2,1,0:T(8,128)(2,1)S(1)} %get-tuple-element.4.received, bf16[3,1,256,2048]{3,2,1,0:T(8,128)(2,1)S(1)} %get-tuple-element.5.grads), custom_call_target="tpu_custom_call" | custom-call | tf_op jit(solution)/shard_map/pallas_call | solution.py:379

commit v10 on v7

--- a/solution.py
+++ b/solution.py
@@ -262,19 +262,25 @@
         def _():
             exchange(g + AHEAD)
 
-        for h in range(GROUP):
-            cols = pl.ds(pl.multiple_of(g * width + h * HEAD_DIM, HEAD_DIM), HEAD_DIM)
-            query, key, value, upstream = stash[0, :, cols], stash[1, :, cols], stash[2, :, cols], up[:, cols]
-            probs = softmax(query, key, bwd_bias[...])
-            grad_value = dot(probs.astype(jnp.bfloat16), upstream, ((0,), (0,)))
-            grad_probs = dot(upstream, value, ((1,), (1,)))
-            center = jnp.sum(probs * grad_probs, axis=-1, keepdims=True)
-            grad_logits = (probs * (grad_probs - center) * SCALE).astype(jnp.bfloat16)
-            grad_query = dot(grad_logits, key, ((1,), (0,)))
-            grad_key = dot(grad_logits, query, ((0,), (0,)))
+        spans = [pl.ds(pl.multiple_of(g * width + h * HEAD_DIM, HEAD_DIM), HEAD_DIM) for h in range(GROUP)]
+        logits = [dot(stash[1, :, cols], stash[0, :, cols], ((1,), (1,))) * SCALE + bwd_bias[...] for cols in spans]
+        grad_probs = [dot(stash[2, :, cols], up[:, cols], ((1,), (1,))) for cols in spans]
+        probs = []
+        for tile in logits:
+            weights = jnp.exp(tile - jnp.max(tile, axis=0, keepdims=True))
+            probs.append(weights * (1.0 / jnp.sum(weights, axis=0, keepdims=True)))
+        for cols, tile in zip(spans, probs):
+            grad_value = dot(tile.astype(jnp.bfloat16), up[:, cols], ((1,), (0,)))
+            grads[2, :, cols] = (grad_value * factor).astype(jnp.bfloat16)
+        grad_logits = []
+        for tile, grad in zip(probs, grad_probs):
+            center = jnp.sum(tile * grad, axis=0, keepdims=True)
+            grad_logits.append((tile * (grad - center) * SCALE).astype(jnp.bfloat16))
+        for cols, tile in zip(spans, grad_logits):
+            grad_key = dot(tile, stash[0, :, cols], ((1,), (0,)))
+            grads[1, :, cols] = (grad_key * factor).astype(jnp.bfloat16)
+            grad_query = dot(tile, stash[1, :, cols], ((0,), (0,)))
             grads[0, :, cols] = (grad_query * factor).astype(jnp.bfloat16)
-            grads[1, :, cols] = (grad_key * factor).astype(jnp.bfloat16)
-            grads[2, :, cols] = (grad_value * factor).astype(jnp.bfloat16)
         send_grads(g).start()
 
     @pl.when(relays)

time: 100 us -> 100 us (level)
  no operation moved by 1% of the time
where the time goes in v10:
time: 100 us
  Pallas kernels  99 us (99%)
  between operations  1.29 us (1%)
    pallas_call x1, Pallas kernels, on_device(): pl.pallas_call(functools.partial(kernel, sections, tensors, replicas), ou...  96.9 us
    pallas_call x1, Pallas kernels, on_device(): pl.pallas_call(store, out_shape=(jax.ShapeDtypeStruct(received.shape, jnp...  2.04 us

profile of v10, /device:TPU:0, one launch (start us, length us, event | category | flops | bytes accessed | tf_op | source)
XLA Modules:
  0.0 100.2 jit_solution(11755935356772792928)
XLA Ops:
  1.3 96.9 %shard_map.77 = (bf16[1,256,2048]{2,1,0:T(8,128)(2,1)S(1)}, bf16[3,1,256,2048]{3,2,1,0:T(8,128)(2,1)S(1)}) custom-call(bf16[3,1,256,2048]{3,2,1,0:T(8,128)(2,1)} %fwd_hbm.1, s32[1,256]{1,0:T(1,128)} %fwd_seg_hbm.1, bf16[3,1,64,8192]{3,2,1,0:T(8,128)(2,1)} %parked_hbm.1, s32[1,256]{1,0:T(1,128)} %bwd_seg_hbm.1, bf16[1,256,2048]{2,1,0:T(8,128)(2,1)} %up_hbm.1, ...), custom_call_target="tpu_custom_call" | custom-call | flops 1879048192 | bytes 11534336 | tf_op jit(solution)/shard_map/pallas_call | solution.py:323
  98.2 2.0 %shard_map.78 = (bf16[1,256,2048]{2,1,0:T(8,128)(2,1)}, bf16[3,1,256,2048]{3,2,1,0:T(8,128)(2,1)}) custom-call(bf16[1,256,2048]{2,1,0:T(8,128)(2,1)S(1)} %get-tuple-element.4.received, bf16[3,1,256,2048]{3,2,1,0:T(8,128)(2,1)S(1)} %get-tuple-element.5.grads), custom_call_target="tpu_custom_call" | custom-call | tf_op jit(solution)/shard_map/pallas_call | solution.py:358
